TPU v7x, 32 devices: a whole 2x2x4 slice. The times are simulated.
32 devices in a mesh: pairs: 8 (over y, x, core), day: 4 (over z).
Axes of the slice: x: 2, y: 2, z: 4, core: 2. Of those that a mesh axis runs over, the one named last changes fastest.
Arguments:
- spectra: bfloat16 [4, 2, 256, 18432], P('day', None, 'pairs'), may hold values from -6 to 6
- station_row: int32 [256], replicated, may hold values from 0 to 255, as said below
- needed: int32 [128], P('pairs'), may hold values from 0 to 255, as said below
- pair_list: int32 [512, 2], P('pairs'), may hold values from 0 to 15, as said below
- counts: int32 [8], P('pairs'), may hold values from 32 to 64, as said below
Outputs:
- correlations: float32 [512, 1024], P(('pairs', 'day'))
Inputs may be any that keep to these rules, and one draw needn't show every extreme that they name: `station_row`: A permutation of the stations: each row of the spectra belongs to exactly one station. `needed`: each block's 16 entries are distinct stations; at most 4 of one block's stations have their rows on any one index of pairs, and in every block some index of pairs holds exactly 4 of them. `pair_list`: the two positions of a slot differ; empty slots also hold valid positions. `counts`: the live slots of a block are its first ones; in every draw some block has all 64 slots live.
All inputs are finite; a program needn't handle non-finite values.
Results may differ from a plain program's by a relative error of at most 0.013.
Values may be sent and summed in bfloat16 or wider, within the bound.
A program may use at most 128 MiB of HBM per device.

v0:
```python
import math
import jax
import jax.numpy as jnp
from jax import lax
from jax.sharding import PartitionSpec as P

F = 18432
LAGS = 1024
KLO = 720
NFFT = 72000
CAP = 4
TWO_PI = 2.0 * math.pi
FLOOR = 0.25


def angle_rows(first_bin, width):
    bins_here = first_bin + jnp.arange(width, dtype=jnp.int32)
    shifts = jnp.arange(LAGS, dtype=jnp.int32) - LAGS // 2
    phases = jnp.mod(bins_here[:, None] * shifts[None, :], NFFT).astype(jnp.float32) * (
        TWO_PI / NFFT
    )
    return (jnp.cos(phases), jnp.sin(phases))


def to_lags(stack_real, stack_imag, bin_start):
    width_all = stack_real.shape[1]
    block_width = math.gcd(width_all, 512)
    low_cos, low_sin = angle_rows(0, block_width)

    def add_block(index, total):
        offset = index * block_width
        high_cos, high_sin = angle_rows(KLO + bin_start + offset, 1)
        cosine = (high_cos * low_cos - high_sin * low_sin).astype(jnp.bfloat16)
        sine = (high_sin * low_cos + high_cos * low_sin).astype(jnp.bfloat16)
        part_real = lax.dynamic_slice_in_dim(stack_real, offset, block_width, 1)
        part_imag = lax.dynamic_slice_in_dim(stack_imag, offset, block_width, 1)
        total = total + jnp.dot(part_real, cosine, preferred_element_type=jnp.float32)
        return total - jnp.dot(part_imag, sine, preferred_element_type=jnp.float32)

    empty = jnp.zeros((stack_real.shape[0], LAGS), jnp.float32)
    total = lax.fori_loop(0, width_all // block_width, add_block, empty)
    return total * (8.0 / math.sqrt(F))


def owner_ranks(owners):
    length = owners.shape[-1]
    earlier = jnp.arange(length)[None, :] < jnp.arange(length)[:, None]
    same = owners[..., :, None] == owners[..., None, :]
    return jnp.sum(jnp.logical_and(same, earlier), axis=-1)


def make_stack(sums, first_slot, live_count, days):
    slots_here = first_slot + jnp.arange(sums.shape[0], dtype=jnp.int32)
    live = (slots_here < live_count).astype(jnp.float32)[:, None]
    coherence = (sums[:, 2] * sums[:, 2] + sums[:, 3] * sums[:, 3]) / (days * days)
    factor = coherence * live
    stack_real = (sums[:, 0] / days * factor).astype(jnp.bfloat16)
    stack_imag = (sums[:, 1] / days * factor).astype(jnp.bfloat16)
    return (stack_real, stack_imag)


def day_terms(left, right):
    cross_real = left[0] * right[0] + left[1] * right[1]
    cross_imag = left[1] * right[0] - left[0] * right[1]
    divisor = jnp.maximum(jnp.sqrt(cross_real * cross_real + cross_imag * cross_imag), FLOOR)
    return jnp.stack([cross_real, cross_imag, cross_real / divisor, cross_imag / divisor], axis=1)


def shards(spectra, station_row, needed, pair_list, counts):
    holders = lax.axis_size("pairs")
    days_here = lax.axis_size("day")
    stations_here = spectra.shape[2]
    slot_count = pair_list.shape[0]
    my_rows = station_row[needed]
    my_owner = my_rows // stations_here
    my_rank = owner_ranks(my_owner)
    my_slot = my_owner * CAP + my_rank
    onehot = my_slot[:, None] == jnp.arange(holders * CAP, dtype=jnp.int32)[None, :]
    asked = jnp.sum(jnp.where(onehot, (my_rows % stations_here)[:, None], 0), axis=0)
    wanted = lax.all_to_all(
        asked.reshape(holders, CAP), "pairs", split_axis=0, concat_axis=0, tiled=True
    )
    day_count = spectra.shape[0]
    bins_all = spectra.shape[3]
    outgoing = jnp.take(spectra, wanted.reshape(-1), axis=2).reshape(
        day_count, 2, holders, CAP, bins_all
    )
    incoming = lax.all_to_all(outgoing, "pairs", split_axis=2, concat_axis=2, tiled=True)
    mine_spec = jnp.take(incoming.reshape(day_count, 2, holders * CAP, bins_all), my_slot, axis=2)
    first = jnp.take(mine_spec, pair_list[:, 0], axis=2)
    second = jnp.take(mine_spec, pair_list[:, 1], axis=2)
    share = slot_count // days_here
    live_count = counts[0]
    left = first[0].astype(jnp.float32)
    right = second[0].astype(jnp.float32)
    sums = lax.psum_scatter(
        day_terms(left, right).astype(jnp.bfloat16), "day", scatter_dimension=0, tiled=True
    ).astype(jnp.float32)
    first_slot = lax.axis_index("day") * share
    stack_real, stack_imag = make_stack(sums, first_slot, live_count, days_here)
    return to_lags(stack_real, stack_imag, 0)


def solution(mesh):
    in_specs = (P("day", None, "pairs", None), P(), P("pairs"), P("pairs", None), P("pairs"))
    out_specs = P(("pairs", "day"), None)
    return jax.shard_map(shards, mesh=mesh, in_specs=in_specs, out_specs=out_specs, check_vma=False)
```

profile of v0, /device:TPU:0, one launch (start us, length us, event | category | flops | bytes accessed | tf_op | source)
XLA Modules:
  0.0 1182.2 jit_solution(6503301249137884689)
XLA Ops:
  37.3 28.6 %all-to-all-done.1 = bf16[1,2,8,4,18432]{4,1,3,0,2:T(2,128)(2,1)S(1)} async-done(((bf16[1,2,8,4,18432]{4,1,3,0,2:T(2,128)(2,1)}), bf16[1,2,8,4,18432]{4,1,3,0,2:T(2,128)(2,1)S(1)}, u32[]{:S(2)}, u32[]{:S(2)}) %all-to-all-start.1) | async-done | bytes 2359328 | tf_op jit(solution)/shard_map/all_to_all | solution.py:88
  70.0 11.8 gather_fusion.3
  81.7 11.8 gather_fusion.4
  93.6 16.3 %fusion.40 = (f32[1,2,64,18432]{3,2,1,0:T(8,128)}, f32[1,2,64,18432]{3,2,1,0:T(8,128)}) fusion(bf16[64,2,18432]{2,1,0:T(2,128)(2,1)} %gather_fusion.4, pred[64]{0:T(512)(128)(4,1)S(1)} %copy-done.3, bf16[64,2,18432]{2,1,0:T(2,128)(2,1)} %gather_fusion.3, pred[64]{0:T(512)(128)(4,1)S(1)} %copy-done.2), kind=kLoop, calls=%fused_computation.49 | loop fusion | flops 9437184 | bytes 28311680 | tf_op jit(solution)/shard_map/convert_element_type | solution.py:95
  130.4 322.2 %all-reduce.3.cloned.1.call-done = bf16[64,4,18432]{2,1,0:T(4,128)(2,1)} async-done(((bf16[64,4,18432]{2,1,0:T(4,128)(2,1)}), bf16[64,4,18432]{2,1,0:T(4,128)(2,1)}) %all-reduce.3.cloned.1.call-update) | async-done | bytes 9437200
  459.7 714.9 %while.19 = (s32[]{:T(128)}, f32[16,1024]{1,0:T(8,128)S(1)}, bf16[16,18432]{1,0:T(8,128)(2,1)S(1)}, bf16[16,18432]{1,0:T(8,128)(2,1)S(1)}, s32[1024]{0:T(1024)S(...) while((s32[]{:T(128)}, f32[16,1024]{1,0:T(8,128)S(1)}, ...), condition=%wide.region_4.6_spmd.clone.clone.clone.clone, body=%wide.region_3.5_spmd.clone.clone.clone.clone.sunk | while | flops 47245320 | bytes 327861 | solution.py:41
  459.8 9.9 convolution_add_fusion.2
  469.7 9.9 convolution_subtract_fusion.2
  479.7 9.9 convolution_add_fusion.2
  489.6 9.9 convolution_subtract_fusion.2
  499.5 9.9 convolution_add_fusion.2
  509.4 9.9 convolution_subtract_fusion.2
  519.4 9.9 convolution_add_fusion.2
  539.2 9.9 convolution_add_fusion.2
  549.2 9.9 convolution_subtract_fusion.2
  559.1 9.9 convolution_add_fusion.2
  569.0 9.9 convolution_subtract_fusion.2
  579.0 9.9 convolution_add_fusion.2
  588.9 9.9 convolution_subtract_fusion.2
  598.8 9.9 convolution_add_fusion.2
  608.7 9.9 convolution_subtract_fusion.2
  618.7 9.9 convolution_add_fusion.2
  628.6 9.9 convolution_subtract_fusion.2
  638.5 9.9 convolution_add_fusion.2
  648.4 9.9 convolution_subtract_fusion.2
  658.4 9.9 convolution_add_fusion.2
  668.3 9.9 convolution_subtract_fusion.2
  678.3 9.9 convolution_add_fusion.2
  688.2 9.9 convolution_subtract_fusion.2
  698.1 9.9 convolution_add_fusion.2
  708.0 9.9 convolution_subtract_fusion.2
  718.0 9.9 convolution_add_fusion.2
  727.9 9.9 convolution_subtract_fusion.2
  737.8 9.9 convolution_add_fusion.2
  747.7 9.9 convolution_subtract_fusion.2
  757.7 9.9 convolution_add_fusion.2
  767.6 9.9 convolution_subtract_fusion.2
  777.5 9.9 convolution_add_fusion.2
  787.4 9.9 convolution_subtract_fusion.2
  797.4 9.9 convolution_add_fusion.2
  807.3 9.9 convolution_subtract_fusion.2
  817.3 9.9 convolution_add_fusion.2
  837.1 9.9 convolution_add_fusion.2
  847.0 9.9 convolution_subtract_fusion.2
  857.0 9.9 convolution_add_fusion.2
  866.9 9.9 convolution_subtract_fusion.2
  876.8 9.9 convolution_add_fusion.2
  886.7 9.9 convolution_subtract_fusion.2
  896.7 9.9 convolution_add_fusion.2
  916.5 9.9 convolution_add_fusion.2
  926.5 9.9 convolution_subtract_fusion.2
  936.4 9.9 convolution_add_fusion.2
  946.3 9.9 convolution_subtract_fusion.2
  956.3 9.9 convolution_add_fusion.2
  976.1 9.9 convolution_add_fusion.2
  996.0 9.9 convolution_add_fusion.2
  1015.8 9.9 convolution_add_fusion.2
  1035.7 9.9 convolution_add_fusion.2
  1055.6 9.9 convolution_add_fusion.2
  1075.4 9.9 convolution_add_fusion.2
  1095.3 9.9 convolution_add_fusion.2
  1115.1 9.9 convolution_add_fusion.2
  1135.0 9.9 convolution_add_fusion.2
  1154.8 9.9 convolution_add_fusion.2
  (105 shorter events, 202.1 us)
Async XLA Ops:
  6.5 0.7 copy-start
  8.9 10.7 all-to-all-start
  32.2 4.6 copy-start.4
  32.2 33.8 %all-to-all-start.1 = ((bf16[1,2,8,4,18432]{4,1,3,0,2:T(2,128)(2,1)}), bf16[1,2,8,4,18432]{4,1,3,0,2:T(2,128)(2,1)S(1)}, u32[]{:S(2)}, u32[]{:S(2)}) async-start(bf16[1,2,8,4,18432]{4,1,3,0,2:T(2,128)(2,1)} %broadcast_select_fusion), calls=%async_computation.1 | async-start | bytes 4718592 | tf_op jit(solution)/shard_map/all_to_all | solution.py:88
  36.5 416.1 %all-reduce.3.cloned.1.call-start = ((), (), s32[]{:S(2)}) async-start(), calls=%async_computation.2 | async-start | bytes 18874368
  81.7 11.8 copy-start.2
  81.7 11.8 copy-start.3
  128.3 0.7 copy-start.5
  1174.6 0.7 copy-start.1
Sparse Core Ops, SparseCore 0:
  128.5 324.0 all-reduce.2
where the time goes:
time: 1180 us
  matrix products  712 us (60%)
  waiting for transfers between devices  351 us (30%)
  local copies, waits for them, and re-layouts  49.7 us (4%)
  other arithmetic  44.2 us (4%)
  between operations  14.9 us (1%)
    dot_general x36, matrix products, add_block(): jnp.dot(part_real, cosine, preferred_element_type=jnp.float32)  357 us
    dot_general x36, matrix products, add_block(): return total - jnp.dot(part_imag, sine, preferred_element_type=jnp.float32)  356 us
    unnamed x2, waiting for transfers between devices  322 us
    all_to_all x1, waiting for transfers between devices, shards(): lax.all_to_all(outgoing, 'pairs', split_axis=2, concat_axis=2, tiled=True)  28.6 us
  transfers between devices with their start and end apart: 3, of which 2 were waited for; matrix products, arithmetic and copies ran while one was open for 1% of the time, Pallas kernels for 0%

commit v1 on v0

--- a/solution.py
+++ b/solution.py
@@ -85,7 +85,12 @@
     outgoing = jnp.take(spectra, wanted.reshape(-1), axis=2).reshape(
         day_count, 2, holders, CAP, bins_all
     )
-    incoming = lax.all_to_all(outgoing, "pairs", split_axis=2, concat_axis=2, tiled=True)
+    incoming = jnp.concatenate(
+        lax.all_to_all(
+            jnp.stack(jnp.split(outgoing, lax.axis_size("pairs"), axis=2)), "pairs", 0, 0
+        ),
+        axis=2,
+    )
     mine_spec = jnp.take(incoming.reshape(day_count, 2, holders * CAP, bins_all), my_slot, axis=2)
     first = jnp.take(mine_spec, pair_list[:, 0], axis=2)
     second = jnp.take(mine_spec, pair_list[:, 1], axis=2)

time: 1180 us -> 1180 us (level)
    convert_element_type x1, other arithmetic: 16.3 us -> 3.04 us  [shards(): right = second[0].astype(jnp.float32)]
where the time goes in v1:
time: 1180 us
  matrix products  712 us (60%)
  waiting for transfers between devices  351 us (30%)
  local copies, waits for them, and re-layouts  57.2 us (5%)
  other arithmetic  34.5 us (3%)
  between operations  14.9 us (1%)
    dot_general x36, matrix products, add_block(): jnp.dot(part_real, cosine, preferred_element_type=jnp.float32)  357 us
    dot_general x36, matrix products, add_block(): return total - jnp.dot(part_imag, sine, preferred_element_type=jnp.float32)  356 us
    unnamed x2, waiting for transfers between devices  322 us
    all_to_all x1, waiting for transfers between devices, shards(): lax.all_to_all(jnp.stack(jnp.split(outgoing, lax.axis_size('pairs'), axis...  28.6 us
  transfers between devices with their start and end apart: 3, of which 2 were waited for; matrix products, arithmetic and copies ran while one was open for 1% of the time, Pallas kernels for 0%

profile of v1, /device:TPU:0, one launch (start us, length us, event | category | flops | bytes accessed | tf_op | source)
XLA Modules:
  0.0 1180.0 jit_solution(1083958754235201050)
XLA Ops:
  43.3 28.6 %all-to-all-done.1 = bf16[8,1,2,1,4,18432]{5,2,4,3,1,0:T(2,128)(2,1)S(1)} async-done(((bf16[8,1,2,1,4,18432]{5,2,4,3,1,0:T(2,128)(2,1)}), bf16[8,1,2,1,4,18432]{5,2,4,3,1,0:T(2,128)(2,1)S(1)}, u32[]{:S(2)}, u32[]{:S(2)}) %all-to-all-start.1) | async-done | bytes 2359328 | tf_op jit(solution)/shard_map/all_to_all | solution.py:89
  75.9 11.9 %gather_fusion.3 = bf16[64,2,18432]{2,1,0:T(2,128)(2,1)} fusion(bf16[2,16,18432]{2,0,1:T(2,128)(2,1)S(1)} %fusion.54, s32[1024]{0:T(1024)S(1)} %get-tuple-element.283), kind=kCustom, calls=%fused_computation.clone | custom fusion | bytes 9437440 | tf_op jit(solution)/shard_map/jit(_take)/gather | solution.py:95
  87.8 11.8 %gather_fusion.4 = bf16[64,2,18432]{2,1,0:T(2,128)(2,1)} fusion(bf16[2,16,18432]{2,0,1:T(2,128)(2,1)S(1)} %fusion.54, s32[1024]{0:T(1024)S(1)} %get-tuple-element.282), kind=kCustom, calls=%fused_computation.1.clone | custom fusion | bytes 9437440 | tf_op jit(solution)/shard_map/jit(_take)/gather | solution.py:96
  128.1 322.3 %all-reduce.3.cloned.1.call-done = bf16[64,4,18432]{2,1,0:T(4,128)(2,1)} async-done(((bf16[64,4,18432]{2,1,0:T(4,128)(2,1)}), bf16[64,4,18432]{2,1,0:T(4,128)(2,1)}) %all-reduce.3.cloned.1.call-update) | async-done | bytes 9437200
  457.6 714.9 %while.19 = (s32[]{:T(128)}, f32[16,1024]{1,0:T(8,128)S(1)}, bf16[16,18432]{1,0:T(8,128)(2,1)S(1)}, bf16[16,18432]{1,0:T(8,128)(2,1)S(1)}, s32[1024]{0:T(1024)S(...) while((s32[]{:T(128)}, f32[16,1024]{1,0:T(8,128)S(1)}, ...), condition=%wide.region_4.6_spmd.clone.clone.clone.clone, body=%wide.region_3.5_spmd.clone.clone.clone.clone.sunk | while | flops 47245320 | bytes 327861 | solution.py:41
  457.7 9.9 convolution_add_fusion.2
  467.6 9.9 convolution_subtract_fusion.2
  477.5 9.9 convolution_add_fusion.2
  497.4 9.9 convolution_add_fusion.2
  507.3 9.9 convolution_subtract_fusion.2
  517.2 9.9 convolution_add_fusion.2
  527.1 9.9 convolution_subtract_fusion.2
  537.1 9.9 convolution_add_fusion.2
  547.0 9.9 convolution_subtract_fusion.2
  557.0 9.9 convolution_add_fusion.2
  566.9 9.9 convolution_subtract_fusion.2
  576.8 9.9 convolution_add_fusion.2
  586.7 9.9 convolution_subtract_fusion.2
  596.7 9.9 convolution_add_fusion.2
  606.6 9.9 convolution_subtract_fusion.2
  616.5 9.9 convolution_add_fusion.2
  626.4 9.9 convolution_subtract_fusion.2
  636.4 9.9 convolution_add_fusion.2
  646.3 9.9 convolution_subtract_fusion.2
  656.3 9.9 convolution_add_fusion.2
  666.2 9.9 convolution_subtract_fusion.2
  676.1 9.9 convolution_add_fusion.2
  686.0 9.9 convolution_subtract_fusion.2
  696.0 9.9 convolution_add_fusion.2
  705.9 9.9 convolution_subtract_fusion.2
  715.8 9.9 convolution_add_fusion.2
  725.7 9.9 convolution_subtract_fusion.2
  735.7 9.9 convolution_add_fusion.2
  745.6 9.9 convolution_subtract_fusion.2
  755.5 9.9 convolution_add_fusion.2
  765.4 9.9 convolution_subtract_fusion.2
  775.4 9.9 convolution_add_fusion.2
  795.3 9.9 convolution_add_fusion.2
  805.2 9.9 convolution_subtract_fusion.2
  815.1 9.9 convolution_add_fusion.2
  825.0 9.9 convolution_subtract_fusion.2
  835.0 9.9 convolution_add_fusion.2
  844.9 9.9 convolution_subtract_fusion.2
  854.8 9.9 convolution_add_fusion.2
  874.7 9.9 convolution_add_fusion.2
  884.6 9.9 convolution_subtract_fusion.2
  894.5 9.9 convolution_add_fusion.2
  904.5 9.9 convolution_subtract_fusion.2
  914.4 9.9 convolution_add_fusion.2
  924.3 9.9 convolution_subtract_fusion.2
  934.3 9.9 convolution_add_fusion.2
  944.2 9.9 convolution_subtract_fusion.2
  954.1 9.9 convolution_add_fusion.2
  964.0 9.9 convolution_subtract_fusion.2
  974.0 9.9 convolution_add_fusion.2
  993.8 9.9 convolution_add_fusion.2
  1013.7 9.9 convolution_add_fusion.2
  1033.6 9.9 convolution_add_fusion.2
  1053.4 9.9 convolution_add_fusion.2
  1073.3 9.9 convolution_add_fusion.2
  1093.1 9.9 convolution_add_fusion.2
  1113.0 9.9 convolution_add_fusion.2
  1132.8 9.9 convolution_add_fusion.2
  1152.7 9.9 convolution_add_fusion.2
  (119 shorter events, 206.2 us)
Async XLA Ops:
  6.5 0.7 copy-start
  8.9 10.7 all-to-all-start
  38.1 4.6 copy-start.7
  38.1 33.8 %all-to-all-start.1 = ((bf16[8,1,2,1,4,18432]{5,2,4,3,1,0:T(2,128)(2,1)}), bf16[8,1,2,1,4,18432]{5,2,4,3,1,0:T(2,128)(2,1)S(1)}, u32[]{:S(2)}, u32[]{:S(2)}) async-start(bf16[8,1,2,1,4,18432]{5,2,4,3,1,0:T(2,128)(2,1)} %fusion.55), calls=%async_computation.1 | async-start | bytes 4718592 | tf_op jit(solution)/shard_map/all_to_all | solution.py:89
  42.4 408.0 %all-reduce.3.cloned.1.call-start = ((), (), s32[]{:S(2)}) async-start(), calls=%async_computation.2 | async-start | bytes 18874368
  87.8 11.8 %copy-start.6 = (pred[64]{0:T(512)(128)(4,1)S(1)}, pred[64]{0:T(512)(128)(4,1)}, u32[]{:S(2)}) copy-start(pred[64]{0:T(512)(128)(4,1)} %get-tuple-element.260) | copy-start | bytes 196
  99.6 5.5 copy-start.2
  99.6 5.5 copy-start.5
  113.0 4.2 copy-start.3
  113.0 4.2 copy-start.4
  126.2 0.7 copy-start.8
  1172.5 0.7 copy-start.1
Sparse Core Ops, SparseCore 0:
  126.3 324.0 all-reduce.2
